TPU v7x, 32 devices: a whole 2x2x4 slice. The times are simulated.
32 devices in a mesh: table: 4 (over x, core), batch: 8 (over z, y).
Axes of the slice: x: 2, y: 2, z: 4, core: 2. Of those that a mesh axis runs over, the one named last changes fastest.
Arguments:
- emb_table: bfloat16 [16384, 256], P('table'), may hold values from -2 to 2
- feature_ids: int32 [256, 1024, 8], P('batch', 'table'), may hold values from 0 to 4095
- projection: bfloat16 [1024, 256], P('table'), may hold values from -0.1875 to 0.1875
- norm_gain: float32 [256], replicated, may hold values from 0.1 to 1.9
- gate_weight: bfloat16 [256, 512], replicated, may hold values from -0.375 to 0.375
- up_weight: bfloat16 [256, 512], replicated, may hold values from -0.375 to 0.375
- down_weight: bfloat16 [512, 256], replicated, may hold values from -0.25 to 0.25
- out_grad: bfloat16 [256, 1024, 256], P(('batch', 'table')), may hold values from -12 to 12
Outputs:
- block_out: bfloat16 [256, 1024, 256], P(('batch', 'table'))
- table_grad: float32 [16384, 256], P(('table', 'batch'))
- projection_grad: float32 [1024, 256], P('table')
- gain_grad: float32 [256], replicated
- gate_grad: float32 [256, 512], replicated
- up_grad: float32 [256, 512], replicated
- down_grad: float32 [512, 256], replicated
Inputs may be any that keep to these rules, and one draw needn't show every extreme that they name: `feature_ids`: an id names a row of the table shard of the device that holds the feature's table.
All inputs are finite; a program needn't handle non-finite values.
Results may differ from a plain program's by a relative error of at most 0.035.
Values may be sent and summed in bfloat16 or wider, within the bound.
A program may use at most 192 MiB of HBM per device.

v0:
```python
import jax
import jax.numpy as jnp
from jax import lax
from jax.sharding import PartitionSpec as P

epsilon = 1e-06


def mlp_forward(interact, norm_gain, gate_weight, up_weight, down_weight):
    mean_sq = jnp.mean(interact * interact, axis=-1, keepdims=True)
    inv_rms = lax.rsqrt(mean_sq + epsilon)
    normed = interact * inv_rms
    scaled = (normed * norm_gain).astype(jnp.bfloat16)
    gate_pre = jnp.dot(scaled, gate_weight, preferred_element_type=jnp.float32)
    up_pre = jnp.dot(scaled, up_weight, preferred_element_type=jnp.float32)
    hidden = (jax.nn.silu(gate_pre) * up_pre).astype(jnp.bfloat16)
    result = jnp.dot(hidden, down_weight, preferred_element_type=jnp.float32).astype(jnp.bfloat16)
    return (result, (inv_rms, normed, scaled, gate_pre, up_pre, hidden))


def contract(left, right, left_dim, right_dim):
    return lax.dot_general(
        left, right, (((left_dim,), (right_dim,)), ((), ())), preferred_element_type=jnp.float32
    )


def mlp_backward(stored, grad_rows, norm_gain, gate_weight, up_weight, down_weight):
    inv_rms, normed, scaled, gate_pre, up_pre, hidden = stored
    hidden_grad = contract(grad_rows, down_weight, 1, 1)
    down_part = contract(hidden, grad_rows, 0, 0)
    sigmoid_gate = jax.nn.sigmoid(gate_pre)
    up_pre_grad = (hidden_grad * jax.nn.silu(gate_pre)).astype(jnp.bfloat16)
    gate_pre_grad = (
        hidden_grad * up_pre * sigmoid_gate * (1.0 + gate_pre * (1.0 - sigmoid_gate))
    ).astype(jnp.bfloat16)
    gate_part = contract(scaled, gate_pre_grad, 0, 0)
    up_part = contract(scaled, up_pre_grad, 0, 0)
    scaled_grad = contract(gate_pre_grad, gate_weight, 1, 1) + contract(
        up_pre_grad, up_weight, 1, 1
    )
    gain_part = jnp.sum(scaled_grad * normed, axis=0)
    inner_term = scaled_grad * norm_gain
    interact_grad = inv_rms * (
        inner_term - normed * jnp.mean(inner_term * normed, axis=-1, keepdims=True)
    )
    return (interact_grad.astype(jnp.bfloat16), gate_part, up_part, down_part, gain_part)


def per_device(
    emb_table, feature_ids, projection, norm_gain, gate_weight, up_weight, down_weight, out_grad
):
    samples_here, feat_here, pool_size = feature_ids.shape
    width = emb_table.shape[1]
    rank_width = projection.shape[1]
    rows_here = emb_table.shape[0]
    shards = lax.axis_size("table")
    picked = jnp.take(emb_table, feature_ids.reshape(-1), axis=0).reshape(
        samples_here, feat_here, pool_size, width
    )
    embeds = jnp.sum(picked, axis=2, dtype=jnp.float32).astype(jnp.bfloat16)
    owned = samples_here // shards
    gathered = lax.all_to_all(embeds, "table", split_axis=0, concat_axis=1, tiled=True)
    inter_own = lax.psum_scatter(
        jnp.einsum("sfd,fk->sdk", embeds, projection, preferred_element_type=jnp.float32).astype(
            jnp.bfloat16
        ),
        "table",
        scatter_dimension=0,
        tiled=True,
    )
    interact = jnp.einsum("sfd,sdk->sfk", gathered, inter_own, preferred_element_type=jnp.float32)
    result, stored = mlp_forward(
        interact.reshape(-1, rank_width), norm_gain, gate_weight, up_weight, down_weight
    )
    block_out = result.reshape(owned, -1, width)
    interact_grad, gate_part, up_part, down_part, gain_part = mlp_backward(
        stored, out_grad.reshape(-1, width), norm_gain, gate_weight, up_weight, down_weight
    )
    grad_owned = interact_grad.reshape(owned, -1, rank_width)
    emb_parts = gathered.reshape(owned, shards, -1, width)
    zgrad_partial = jnp.einsum(
        "stfd,stfk->stdk",
        emb_parts,
        grad_owned.reshape(owned, shards, -1, rank_width),
        preferred_element_type=jnp.float32,
    )
    rounded = lax.optimization_barrier(zgrad_partial.astype(jnp.bfloat16)).astype(jnp.float32)
    inter_grad_own = jnp.sum(rounded, axis=1).astype(jnp.bfloat16)
    term_owned = jnp.einsum(
        "sfk,sdk->sfd", grad_owned, inter_own, preferred_element_type=jnp.float32
    )
    local_term = lax.all_to_all(
        term_owned.astype(jnp.bfloat16), "table", split_axis=1, concat_axis=0, tiled=True
    ).astype(term_owned.dtype)
    inter_grad = lax.all_gather(inter_grad_own, "table", axis=0, tiled=True)
    embed_grad = (
        local_term
        + jnp.einsum("fk,sdk->sfd", projection, inter_grad, preferred_element_type=jnp.float32)
    ).astype(jnp.bfloat16)
    proj_part = jnp.einsum("sfd,sdk->fk", embeds, inter_grad, preferred_element_type=jnp.float32)
    projection_grad = lax.psum(proj_part.astype(jnp.bfloat16), "batch").astype(jnp.float32)
    gate_grad, up_grad, down_grad, gain_grad = lax.psum(
        (gate_part, up_part, down_part, gain_part), ("table", "batch")
    )
    spread = jnp.broadcast_to(
        embed_grad.astype(jnp.float32)[:, :, None, :], (samples_here, feat_here, pool_size, width)
    )
    table_term = jax.ops.segment_sum(
        spread.reshape(-1, width), feature_ids.reshape(-1), num_segments=rows_here
    )
    table_grad = lax.psum_scatter(
        table_term.astype(jnp.bfloat16), "batch", scatter_dimension=0, tiled=True
    ).astype(jnp.float32)
    return (block_out, table_grad, projection_grad, gain_grad, gate_grad, up_grad, down_grad)


def solution(mesh):
    return jax.shard_map(
        per_device,
        mesh=mesh,
        in_specs=(
            P("table", None),
            P("batch", "table", None),
            P("table", None),
            P(),
            P(),
            P(),
            P(),
            P(("batch", "table"), None, None),
        ),
        out_specs=(
            P(("batch", "table"), None, None),
            P(("table", "batch"), None),
            P("table", None),
            P(),
            P(),
            P(),
            P(),
        ),
        check_vma=False,
    )
```

profile of v0, /device:TPU:0, one launch (start us, length us, event | category | flops | bytes accessed | tf_op | source)
XLA Modules:
  0.0 1184.1 jit_solution(8151774892644249786)
XLA Ops:
  7.2 1.2 compare_and_fusion
  8.4 3.5 copy.29
  11.9 1.7 copy.28
  13.6 4.4 reshape.101
  18.0 0.3 compare_select_fusion
  18.3 257.8 %gather_fusion = bf16[65536,256]{1,0:T(8,128)(2,1)} fusion(bf16[4096,256]{1,0:T(8,128)(2,1)S(1)} %copy-done, s32[65536]{0:T(1024)S(1)} %broadcast_clamp_fusion), kind=kCustom, calls=%fused_computation | custom fusion | bytes 67371008 | tf_op jit(solution)/shard_map/jit(_take)/gather | solution.py:57
  276.1 25.8 %select_reduce_fusion = bf16[32,256,256]{2,1,0:T(8,128)(2,1)} fusion(pred[32,256,8]{2,1,0:T(8,128)(4,1)S(1)} %copy.28, bf16[65536,256]{1,0:T(8,128)(2,1)} %gather_fusion), kind=kLoop, calls=%fused_computation.2 | loop fusion | flops 31457280 | bytes 37814272 | tf_op jit(solution)/shard_map/reduce_sum | solution.py:60
  302.0 5.5 convolution_convert_fusion.2
  307.5 0.0 all-gather.2.cloned.1.call-start
  307.5 77.2 %all_to_all.27 = bf16[32,256,256]{2,1,0:T(8,128)(2,1)} all-to-all(bf16[32,256,256]{2,1,0:T(8,128)(2,1)} %select_reduce_fusion), channel_id=1, replica_groups=mesh['table'=4,'batch'=8] {'table'}, dimensions={0} | all-to-all | bytes 8388608 | tf_op jit(solution)/shard_map/all_to_all | solution.py:62
  384.7 6.5 copy.30
  391.2 4.6 copy.31
  395.7 3.9 multiply_reduce_fusion.2
  399.7 1.8 multiply_convert_fusion.4
  401.6 8.1 fusion.14
  409.6 8.1 fusion.13
  417.7 21.5 %multiply_convert_fusion = (bf16[8192,512]{1,0:T(8,128)(2,1)}, bf16[8192,512]{1,0:T(8,128)(2,1)}, bf16[8192,512]{1,0:T(8,128)(2,1)}) fusion(f32[8192,512]{1,0:T(8,128)} %fusion.13, f32[8192,512]{1,0:T(8,128)} %fusion.14, bf16[8192,256]{1,0:T(8,128)(2,1)S(1)} %bitcast.91, bf16[512,256]{1,0:T(8,128)(2,1)S(1)} %copy-done.14), kind=kOutput, calls=%fused_computation.3 | convolution fusion | flops 2210398208 | bytes 63176704 | tf_op jit(solution)/shard_map/dot_general | solution.py:22
  439.3 9.1 fusion.15
  448.4 10.1 multiply_reduce_fusion
  458.5 7.3 multiply_convert_fusion.3
  465.9 1.9 copy-done.5
  467.8 3.3 fusion.5
  471.1 4.1 reduce_sum.54
  475.2 3.5 convolution_convert_fusion.1
  478.7 4.4 copy.34
  483.1 5.1 all-to-all-start.1
  488.2 3.6 reshape.119
  491.9 62.5 %all-to-all-done.1 = bf16[8,1024,256]{2,0,1:T(8,128)(2,1)} async-done(((bf16[8,1024,256]{2,0,1:T(8,128)(2,1)}), bf16[8,1024,256]{2,0,1:T(8,128)(2,1)}, u32[]{:S(2)}, u32[]{:S(2)}) %all-to-all-start.1) | async-done | bytes 4194336 | tf_op jit(solution)/shard_map/all_to_all | solution.py:92
  554.4 8.7 copy.35
  563.1 5.4 fusion.10
  568.5 0.2 reduce-scatter.5.cloned.1.call-start
  568.7 9.2 fusion.2
  577.9 9.0 copy.36
  586.9 23.8 %broadcast_in_dim.26 = f32[32,256,8,256]{3,2,1,0:T(8,128)} broadcast(f32[32,256,256]{2,1,0:T(8,128)} %copy.36), dimensions={0,1,3} | broadcast | bytes 75497472 | tf_op jit(solution)/shard_map/broadcast_in_dim | solution.py:105
  610.6 351.3 %scatter_custom_fusion = f32[4096,256]{1,0:T(8,128)} fusion(s32[65536]{0:T(1024)S(1)} %reshape.119, f32[65536,256]{1,0:T(8,128)} %bitcast.16, f32[]{:T(128)} %constant.29.clone.1), kind=kCustom, calls=%fused_computation.24 | custom fusion | flops 16777216 | bytes 4194816 | tf_op jit(solution)/shard_map/scatter-add | solution.py:108
  962.0 3.7 convert_element_type.76
  965.8 40.1 %psum.36 = f32[256]{0:T(256)} all-reduce(f32[256]{0:T(256)S(1)} %get-tuple-element.7), channel_id=1, replica_groups=mesh['table'=4,'batch'=8] {'table','batch'}, use_global_device_ids=true, to_apply=%region_9.10 | all-reduce | flops 256 | bytes 2048 | tf_op jit(solution)/shard_map/psum | solution.py:102
  1005.8 8.0 fusion.17
  1013.8 6.7 fusion.16
  1020.5 3.2 fusion.18
  1023.7 7.9 convolution_convert_fusion
  1031.7 1.6 convert_element_type.79
  1033.3 0.4 reduce-scatter.5.cloned.1.call-done
  1033.7 1.8 convert_element_type.77
  1035.5 136.3 %all-reduce.6.cloned.1.call-done = (f32[256,512]{1,0:T(8,128)}, f32[256,512]{1,0:T(8,128)}, f32[512,256]{1,0:T(8,128)}) async-done(((f32[256,512]{1,0:T(8,128)}, f32[256,512]{1,0:T(8,128)}, f32[512,256]{1,0:T(8,128)}), (f32[256,512]{1,0:T(8,128)}, f32[256,512]{1,0:T(8,128)}, f32[512,256]{1,0:T(8,128)})) %all-reduce.6.cloned.1.call-update) | async-done | bytes 1572880 | tf_op jit(solution)/shard_map/psum | solution.py:102
  1171.8 1.9 copy.46
  1173.7 1.9 copy.47
  1175.5 1.9 copy.48
  (54 shorter events, 0.4 us)
Async XLA Ops:
  7.2 11.1 copy-start
  7.2 388.6 %reduce-scatter.3.cloned.1.call-start = ((), (), s32[]{:S(2)}) async-start(), calls=%async_computation.4 | async-start | bytes 5242880 | tf_op jit(solution)/shard_map/reduce_scatter | solution.py:63
  276.1 25.9 %copy-start.12 = (bf16[256,256]{1,0:T(8,128)(2,1)S(1)}, bf16[256,256]{1,0:T(8,128)(2,1)}, u32[]{:S(2)}) copy-start(bf16[256,256]{1,0:T(8,128)(2,1)} %param.10) | copy-start | bytes 393220
  307.5 255.6 %all-gather.2.cloned.1.call-start = ((), (), s32[]{:S(2)}) async-start(), calls=%async_computation.5 | async-start | bytes 5242880 | tf_op jit(solution)/shard_map/all_gather | solution.py:95
  395.7 3.9 copy-start.13
  399.6 10.0 copy-start.2
  399.6 1.9 copy-start.11
  401.5 8.1 copy-start.3
  401.5 8.1 copy-start.10
  409.6 8.1 copy-start.7
  409.6 8.1 copy-start.14
  439.3 9.1 slice-start
  439.3 9.1 slice-start.1
  458.5 9.3 copy-start.6
  465.8 2.0 copy-start.5
  467.8 7.4 copy-start.9
  483.1 71.3 %all-to-all-start.1 = ((bf16[8,1024,256]{2,0,1:T(8,128)(2,1)}), bf16[8,1024,256]{2,0,1:T(8,128)(2,1)}, u32[]{:S(2)}, u32[]{:S(2)}) async-start(bf16[8,1024,256]{2,0,1:T(8,128)(2,1)} %copy.34), calls=%async_computation.2 | async-start | bytes 8388608 | tf_op jit(solution)/shard_map/all_to_all | solution.py:92
  488.2 543.5 %all-reduce.4.cloned.1.call-start = ((), (), s32[]{:S(2)}) async-start(), calls=%async_computation.7 | async-start | bytes 262144 | tf_op jit(solution)/shard_map/psum | solution.py:101
  568.5 465.3 %reduce-scatter.5.cloned.1.call-start = ((), (), s32[]{:S(2)}) async-start(), calls=%async_computation.6 | async-start | bytes 2359296 | tf_op jit(solution)/shard_map/reduce_scatter | solution.py:111
  965.7 206.1 %all-reduce.6.cloned.1.call-start = ((), (), s32[]{:S(2)}) async-start(), calls=%async_computation.8 | async-start | bytes 3145728 | tf_op jit(solution)/shard_map/psum | solution.py:102
  1005.8 8.0 copy-start.4
  1005.8 14.7 %slice-start.2 = ((s8[8388608]{0:T(1024)(128)(4,1)}), s8[4194304]{0:T(1024)(128)(4,1)S(1)}, s32[]{:S(2)}) async-start(s8[8388608]{0:T(1024)(128)(4,1)} %bitcast.88), calls=%async_computation.11 | async-start | bytes 8388608
  1013.8 6.7 slice-start.3
  1013.8 6.7 copy-start.8
  1023.7 153.7 %copy-start.1 = (bf16[4096,256]{1,0:T(8,128)(2,1)S(1)}, bf16[4096,256]{1,0:T(8,128)(2,1)}, u32[]{:S(2)}) copy-start(bf16[4096,256]{1,0:T(8,128)(2,1)} %param.8) | copy-start | bytes 6291460
Sparse Core Ops, SparseCore 0:
  307.6 70.2 reduce-scatter.2
  475.3 53.6 all-gather.1
  568.6 69.5 all-reduce.3
  965.8 67.8 reduce-scatter.4
  1039.8 131.9 all-reduce.5
where the time goes:
time: 1190 us; the launch traced here: 1180 us
  other arithmetic  399 us (34%)
  local copies, waits for them, and re-layouts  336 us (28%)
  waiting for transfers between devices  199 us (17%)
  blocking collectives  117 us (10%)
  matrix products  113 us (9%)
  between operations  14.2 us (1%)
    scatter-add x1, other arithmetic, per_device(): jax.ops.segment_sum(spread.reshape(-1, width), feature_ids.reshape(-1), n...  351 us
    gather x1, local copies, waits for them, and re-layouts, per_device(): jnp.take(emb_table, feature_ids.reshape(-1), axis=0)  258 us
    psum x1, waiting for transfers between devices, per_device(): lax.psum((gate_part, up_part, down_part, gain_part), ('table', 'batch'))  136 us
    all_to_all x1, blocking collectives, per_device(): lax.all_to_all(embeds, 'table', split_axis=0, concat_axis=1, tiled=True)  77.2 us
    all_to_all x1, waiting for transfers between devices, per_device(): lax.all_to_all(term_owned.astype(jnp.bfloat16), 'table', split_axis=1, co...  62.5 us
    dot_general x6, matrix products, contract(): lax.dot_general(left, right, (((left_dim,), (right_dim,)), ((), ())), pre...  58.6 us
    psum x1, blocking collectives, per_device(): lax.psum((gate_part, up_part, down_part, gain_part), ('table', 'batch'))  40.1 us
    reduce_sum x1, other arithmetic, per_device(): embeds = jnp.sum(picked, axis=2, dtype=jnp.float32).astype(jnp.bfloat16)  25.8 us
  transfers between devices with their start and end apart: 6, of which 3 were waited for; matrix products, arithmetic and copies ran while one was open for 39% of the time, Pallas kernels for 0%

commit v1 on v0

v1 whole, which is shorter than its diff:
```python
import functools

import jax
import jax.numpy as jnp
import numpy as np
from jax import lax
from jax.experimental import pallas as pl
from jax.experimental.pallas import tpu as pltpu
from jax.sharding import PartitionSpec as P

epsilon = 1e-06
LANES = 128
DIGITS = 8
VMEM_LIMIT = 56 * 1024 * 1024


def contract(left, right, left_dim, right_dim):
    return lax.dot_general(
        left, right, (((left_dim,), (right_dim,)), ((), ())), preferred_element_type=jnp.float32
    )


def row_scale(rows):
    digit = (np.arange(rows) // LANES) % DIGITS
    digit = np.where(digit == DIGITS - 1, 0, digit)
    return jnp.asarray(2.0 ** (-4.0 * digit), jnp.float32)


def lookup_kernel(ids_ref, table_ref, emb_ref, count_ref):
    tile, pool = ids_ref.shape
    rows = count_ref.shape[1]
    groups = rows // (LANES * DIGITS)
    sub = 8
    for start in range(0, tile, sub):
        ids = ids_ref[pl.ds(start, sub), :]
        lane = lax.broadcasted_iota(jnp.int32, (sub, LANES), 1)
        hi = lax.shift_right_logical(ids, 7)
        value = lax.shift_left(jnp.ones_like(ids), 4 * (hi & 7))
        key = (ids & 127) | (lax.shift_right_logical(hi, 3) << 7)
        acc = [jnp.zeros((sub, LANES), jnp.int32) for _ in range(groups)]
        for p in range(pool):
            key_p = jnp.broadcast_to(key[:, p : p + 1], (sub, LANES)) - lane
            value_p = jnp.broadcast_to(value[:, p : p + 1], (sub, LANES))
            for g in range(groups):
                acc[g] = acc[g] + jnp.where(key_p == g * LANES, value_p, 0)
        for g in range(groups):
            for digit in range(DIGITS):
                if digit == DIGITS - 1:
                    part = lax.shift_right_logical(acc[g], 4 * digit)
                else:
                    part = acc[g] & (15 << (4 * digit))
                column = (g * DIGITS + digit) * LANES
                count_ref[pl.ds(start, sub), pl.ds(column, LANES)] = part.astype(
                    jnp.float32
                ).astype(jnp.bfloat16)
    emb_ref[...] = jnp.dot(
        count_ref[...], table_ref[...], preferred_element_type=jnp.float32
    ).astype(jnp.bfloat16)


def lookup(ids, table):
    total, pool = ids.shape
    rows, width = table.shape
    tile = min(256, total)
    return pl.pallas_call(
        lookup_kernel,
        grid=(total // tile,),
        in_specs=[
            pl.BlockSpec((tile, pool), lambda i: (i, 0)),
            pl.BlockSpec((rows, width), lambda i: (0, 0)),
        ],
        out_specs=[
            pl.BlockSpec((tile, width), lambda i: (i, 0)),
            pl.BlockSpec((tile, rows), lambda i: (i, 0)),
        ],
        out_shape=[
            jax.ShapeDtypeStruct((total, width), jnp.bfloat16),
            jax.ShapeDtypeStruct((total, rows), jnp.bfloat16),
        ],
        compiler_params=pltpu.CompilerParams(vmem_limit_bytes=VMEM_LIMIT),
        cost_estimate=pl.CostEstimate(
            flops=2 * total * rows * width,
            bytes_accessed=total * rows * 2 + total * width * 2 + rows * width * 2,
            transcendentals=0,
        ),
        name="lookup",
    )(ids, table)


def sample_kernel(shards, me_ref, *refs):
    x_refs = refs[:shards]
    proj_ref, gain_ref, gate_ref, up_ref, down_ref, og_ref = refs[shards : shards + 6]
    out_ref = refs[shards + 6]
    eg_refs = refs[shards + 7 : 2 * shards + 7]
    proj_acc, gate_acc, up_acc, down_acc, gain_acc = refs[2 * shards + 7 : 2 * shards + 12]
    xs, igs, egs = refs[2 * shards + 12 :]
    me = me_ref[0]
    feat_here = x_refs[0].shape[1]
    features = xs.shape[0]

    @pl.when(pl.program_id(0) == 0)
    def _():
        for acc in (proj_acc, gate_acc, up_acc, down_acc, gain_acc):
            acc[...] = jnp.zeros_like(acc)

    for j in range(shards):
        first = pl.multiple_of((me ^ j) * feat_here, feat_here)
        xs[pl.ds(first, feat_here), :] = x_refs[j][0]
    inter = contract(xs[...], proj_ref[...], 0, 0).astype(jnp.bfloat16)
    gain = gain_ref[...]
    block = min(256, features)
    for start in range(0, features, block):
        rows = pl.ds(start, block)
        interact = jnp.dot(xs[rows, :], inter, preferred_element_type=jnp.float32)
        inv_rms = lax.rsqrt(jnp.mean(interact * interact, axis=-1, keepdims=True) + epsilon)
        normed = interact * inv_rms
        scaled = (normed * gain).astype(jnp.bfloat16)
        gate_pre = jnp.dot(scaled, gate_ref[...], preferred_element_type=jnp.float32)
        up_pre = jnp.dot(scaled, up_ref[...], preferred_element_type=jnp.float32)
        sig = jax.nn.sigmoid(gate_pre)
        silu = gate_pre * sig
        hidden = (silu * up_pre).astype(jnp.bfloat16)
        out_ref[0, rows, :] = jnp.dot(
            hidden, down_ref[...], preferred_element_type=jnp.float32
        ).astype(jnp.bfloat16)
        og = og_ref[0, rows, :]
        hidden_grad = contract(og, down_ref[...], 1, 1)
        down_acc[...] += contract(hidden, og, 0, 0)
        up_grad = (hidden_grad * silu).astype(jnp.bfloat16)
        gate_grad = (hidden_grad * up_pre * (sig + silu * (1.0 - sig))).astype(jnp.bfloat16)
        gate_acc[...] += contract(scaled, gate_grad, 0, 0)
        up_acc[...] += contract(scaled, up_grad, 0, 0)
        scaled_grad = contract(gate_grad, gate_ref[...], 1, 1) + contract(
            up_grad, up_ref[...], 1, 1
        )
        prod = scaled_grad * normed
        gain_acc[...] += jnp.sum(prod, axis=0, keepdims=True)
        mean = jnp.mean(prod * gain, axis=-1, keepdims=True)
        igs[rows, :] = (inv_rms * (scaled_grad * gain - normed * mean)).astype(jnp.bfloat16)
    inter_grad = contract(xs[...], igs[...], 0, 0).astype(jnp.bfloat16)
    egs[...] = (
        contract(igs[...], inter, 1, 1) + contract(proj_ref[...], inter_grad, 1, 1)
    ).astype(jnp.bfloat16)
    for j in range(shards):
        first = pl.multiple_of((me ^ j) * feat_here, feat_here)
        eg_refs[j][0] = egs[pl.ds(first, feat_here), :]
    proj_acc[...] += jnp.dot(xs[...], inter_grad, preferred_element_type=jnp.float32)


def samples_step(me, parts, proj, gain, gate, up, down, out_grad):
    shards = len(parts)
    owned, feat_here, width = parts[0].shape
    features, rank = proj.shape
    hidden = gate.shape[1]
    whole = lambda s, m: (0, 0)
    per_sample = lambda s, m: (s, 0, 0)
    part_spec = pl.BlockSpec((1, feat_here, width), per_sample)
    sums = [(features, rank), (rank, hidden), (rank, hidden), (hidden, width), (1, rank)]
    rows = owned * features
    return pl.pallas_call(
        functools.partial(sample_kernel, shards),
        grid_spec=pltpu.PrefetchScalarGridSpec(
            num_scalar_prefetch=1,
            grid=(owned,),
            in_specs=[part_spec] * shards
            + [
                pl.BlockSpec((features, rank), whole),
                pl.BlockSpec((1, rank), whole),
                pl.BlockSpec((rank, hidden), whole),
                pl.BlockSpec((rank, hidden), whole),
                pl.BlockSpec((hidden, width), whole),
                pl.BlockSpec((1, features, width), per_sample),
            ],
            out_specs=[pl.BlockSpec((1, features, width), per_sample)]
            + [part_spec] * shards
            + [pl.BlockSpec(shape, whole) for shape in sums],
            scratch_shapes=[
                pltpu.VMEM((features, width), jnp.bfloat16),
                pltpu.VMEM((features, rank), jnp.bfloat16),
                pltpu.VMEM((features, width), jnp.bfloat16),
            ],
        ),
        out_shape=[jax.ShapeDtypeStruct((owned, features, width), jnp.bfloat16)]
        + [jax.ShapeDtypeStruct((owned, feat_here, width), jnp.bfloat16)] * shards
        + [jax.ShapeDtypeStruct(shape, jnp.float32) for shape in sums],
        compiler_params=pltpu.CompilerParams(vmem_limit_bytes=VMEM_LIMIT),
        cost_estimate=pl.CostEstimate(
            flops=2 * rows * rank * (9 * hidden + 6 * width),
            bytes_accessed=rows * width * 8,
            transcendentals=rows * hidden,
        ),
        name="samples",
    )(me, *parts, proj, gain, gate, up, down, out_grad)


def scatter_kernel(shards, *refs):
    eg_refs, count_refs = refs[:shards], refs[shards : 2 * shards]
    scale_ref, out_ref = refs[2 * shards :]
    total = contract(eg_refs[0][...], count_refs[0][...], 0, 0)
    for j in range(1, shards):
        total = total + contract(eg_refs[j][...], count_refs[j][...], 0, 0)
    out_ref[...] = (total * scale_ref[...]).T.astype(jnp.bfloat16)


def scatter(grads, counts, scale):
    shards = len(grads)
    total, width = grads[0].shape
    rows = counts[0].shape[1]
    block = min(512, rows)
    return pl.pallas_call(
        functools.partial(scatter_kernel, shards),
        grid=(rows // block,),
        in_specs=[pl.BlockSpec((total, width), lambda i: (0, 0))] * shards
        + [pl.BlockSpec((total, block), lambda i: (0, i))] * shards
        + [pl.BlockSpec((1, block), lambda i: (0, i))],
        out_specs=pl.BlockSpec((block, width), lambda i: (i, 0)),
        out_shape=jax.ShapeDtypeStruct((rows, width), jnp.bfloat16),
        compiler_params=pltpu.CompilerParams(vmem_limit_bytes=VMEM_LIMIT),
        cost_estimate=pl.CostEstimate(
            flops=2 * shards * total * rows * width,
            bytes_accessed=shards * total * (rows + width) * 2,
            transcendentals=0,
        ),
        name="scatter",
    )(*grads, *counts, scale)


def per_device(
    shards,
    emb_table,
    feature_ids,
    projection,
    norm_gain,
    gate_weight,
    up_weight,
    down_weight,
    out_grad,
):
    samples_here, feat_here, pool_size = feature_ids.shape
    rows_here, width = emb_table.shape
    owned = samples_here // shards
    me = lax.axis_index("table")
    scale = row_scale(rows_here)
    table = (emb_table.astype(jnp.float32) * scale[:, None]).astype(jnp.bfloat16)
    proj = lax.all_gather(projection, "table", axis=0, tiled=True)

    swap = lambda value, j: lax.ppermute(value, "table", [(i, i ^ j) for i in range(shards)])
    parts, counts = [None] * shards, [None] * shards
    for j in reversed(range(shards)):
        ids = lax.dynamic_slice_in_dim(feature_ids, (me ^ j) * owned, owned, 0)
        embeds, counts[j] = lookup(ids.reshape(-1, pool_size), table)
        embeds = embeds.reshape(owned, feat_here, width)
        parts[j] = embeds if j == 0 else swap(embeds, j)
    results = samples_step(
        me[None].astype(jnp.int32),
        parts,
        proj,
        norm_gain[None, :],
        gate_weight,
        up_weight,
        down_weight,
        out_grad,
    )
    block_out = results[0]
    grads = [
        (g if j == 0 else swap(g, j)).reshape(-1, width)
        for j, g in enumerate(results[1 : shards + 1])
    ]
    proj_part, gate_part, up_part, down_part, gain_part = results[shards + 1 :]
    table_term = scatter(grads, counts, scale[None, :])
    table_grad = lax.psum_scatter(
        table_term, "batch", scatter_dimension=0, tiled=True
    ).astype(jnp.float32)
    proj_own = lax.psum_scatter(
        proj_part.astype(jnp.bfloat16), "table", scatter_dimension=0, tiled=True
    )
    projection_grad = lax.psum(proj_own, "batch").astype(jnp.float32)
    gate_grad, up_grad, down_grad, gain_grad = lax.psum(
        (gate_part, up_part, down_part, gain_part), ("table", "batch")
    )
    return (
        block_out,
        table_grad,
        projection_grad,
        gain_grad[0],
        gate_grad,
        up_grad,
        down_grad,
    )


def solution(mesh):
    shards = mesh.shape["table"]
    return jax.shard_map(
        functools.partial(per_device, shards),
        mesh=mesh,
        in_specs=(
            P("table", None),
            P("batch", "table", None),
            P("table", None),
            P(),
            P(),
            P(),
            P(),
            P(("batch", "table"), None, None),
        ),
        out_specs=(
            P(("batch", "table"), None, None),
            P(("table", "batch"), None),
            P("table", None),
            P(),
            P(),
            P(),
            P(),
        ),
        check_vma=False,
    )
```

time: 1190 us -> 468 us (0.39)
  other arithmetic: 399 us -> 8.37 us
  local copies, waits for them, and re-layouts: 336 us -> 14.5 us
  Pallas kernels: 0 us -> 140 us
  matrix products: 113 us -> 0 us
  blocking collectives: 117 us -> 55 us
  waiting for transfers between devices: 199 us -> 230 us
    scatter-add x1 -> x0, other arithmetic: 351 us -> none  [per_device(): jax.ops.segment_sum(spread.reshape(-1, width), feature_ids.reshape(-1), n...]
    gather x1 -> x0, local copies, waits for them, and re-layouts: 258 us -> none  [per_device(): jnp.take(emb_table, feature_ids.reshape(-1), axis=0)]
    pallas_call x0 -> x6, Pallas kernels: none -> 140 us  [the longest x4 63.6 us: lookup(): pl.pallas_call(lookup_kernel, grid=(total // tile,), in_specs=[pl.BlockSp...]
    dot_general x15 -> x0, matrix products: 113 us -> none  [the longest x6 58.6 us: contract(): lax.dot_general(left, right, (((left_dim,), (right_dim,)), ((), ())), pre...]
    all_to_all x1 -> x0, blocking collectives: 77.2 us -> none  [per_device(): lax.all_to_all(embeds, 'table', split_axis=0, concat_axis=1, tiled=True)]
    reduce_scatter x2, waiting for transfers between devices: 0.45 us -> 69 us  [the longest x1 45 us: per_device(): lax.psum_scatter(table_term, 'batch', scatter_dimension=0, tiled=True)]
    all_to_all x1 -> x0, waiting for transfers between devices: 62.5 us -> none  [per_device(): lax.all_to_all(term_owned.astype(jnp.bfloat16), 'table', split_axis=1, co...]
    reduce_sum x2 -> x0, other arithmetic: 30 us -> none  [the longest x1 25.8 us: per_device(): embeds = jnp.sum(picked, axis=2, dtype=jnp.float32).astype(jnp.bfloat16)]
  transfers between devices with their start and end apart: 6 -> 10, of which waited for: 3 -> 5; matrix products, arithmetic and copies ran while one was open for 39% -> 2% of each run, Pallas kernels for 0% -> 17%
where the time goes in v1:
time: 468 us
  waiting for transfers between devices  230 us (49%)
  Pallas kernels  140 us (30%)
  blocking collectives  55 us (12%)
  local copies, waits for them, and re-layouts  14.5 us (3%)
  between operations  13.9 us (3%)
  other arithmetic  8.37 us (2%)
  starting transfers between devices  5.94 us (1%)
    psum x1, waiting for transfers between devices, per_device(): lax.psum((gate_part, up_part, down_part, gain_part), ('table', 'batch'))  136 us
    pallas_call x4, Pallas kernels, lookup(): pl.pallas_call(lookup_kernel, grid=(total // tile,), in_specs=[pl.BlockSp...  63.6 us
    pallas_call x1, Pallas kernels, samples_step(): pl.pallas_call(functools.partial(sample_kernel, shards), grid_spec=pltpu....  45.8 us
    reduce_scatter x1, waiting for transfers between devices, per_device(): lax.psum_scatter(table_term, 'batch', scatter_dimension=0, tiled=True)  45 us
    psum x1, blocking collectives, per_device(): lax.psum((gate_part, up_part, down_part, gain_part), ('table', 'batch'))  41 us
    pallas_call x1, Pallas kernels, scatter(): pl.pallas_call(functools.partial(scatter_kernel, shards), grid=(rows // b...  30.4 us
    ppermute x6, waiting for transfers between devices, per_device(): lax.ppermute(value, 'table', [(i, i ^ j) for i in range(shards)])  24.4 us
    reduce_scatter x1, waiting for transfers between devices, per_device(): lax.psum_scatter(proj_part.astype(jnp.bfloat16), 'table', scatter_dimensi...  24 us
  transfers between devices with their start and end apart: 10, of which 5 were waited for; matrix products, arithmetic and copies ran while one was open for 2% of the time, Pallas kernels for 17%

profile of v1, /device:TPU:0, one launch (start us, length us, event | category | flops | bytes accessed | tf_op | source)
XLA Modules:
  0.0 467.7 jit_solution(16654784828433303091)
XLA Ops:
  7.2 0.0 reduce-scatter.5.cloned.1.call-start
  7.2 1.0 constant_dynamic-slice_fusion
  8.2 1.3 copy.19
  9.5 2.9 multiply_convert_fusion.table_ref
  12.4 15.9 %lookup.7 = (bf16[2048,256]{1,0:T(8,128)(2,1)}, bf16[2048,4096]{1,0:T(8,128)(2,1)}) custom-call(s32[2048,8]{1,0:T(8,128)} %bitcast.19, bf16[4096,256]{1,0:T(8,128)(2,1)} %multiply_convert_fusion.table_ref), custom_call_target="tpu_custom_call" | custom-call | flops 4294967296 | bytes 19922944 | tf_op jit(solution)/shard_map/lookup/pallas_call | solution.py:65
  28.3 2.4 collective-permute-start.2
  30.7 1.3 copy.18
  32.0 15.9 %lookup.6 = (bf16[2048,256]{1,0:T(8,128)(2,1)}, bf16[2048,4096]{1,0:T(8,128)(2,1)}) custom-call(s32[2048,8]{1,0:T(8,128)} %bitcast.21, bf16[4096,256]{1,0:T(8,128)(2,1)} %multiply_convert_fusion.table_ref), custom_call_target="tpu_custom_call" | custom-call | flops 4294967296 | bytes 19922944 | tf_op jit(solution)/shard_map/lookup/pallas_call | solution.py:65
  47.9 0.6 collective-permute-start.1
  48.5 1.3 copy.17
  49.8 15.9 %lookup.5 = (bf16[2048,256]{1,0:T(8,128)(2,1)}, bf16[2048,4096]{1,0:T(8,128)(2,1)}) custom-call(s32[2048,8]{1,0:T(8,128)} %bitcast.22, bf16[4096,256]{1,0:T(8,128)(2,1)} %multiply_convert_fusion.table_ref), custom_call_target="tpu_custom_call" | custom-call | flops 4294967296 | bytes 19922944 | tf_op jit(solution)/shard_map/lookup/pallas_call | solution.py:65
  65.8 0.1 collective-permute-start
  65.9 1.3 copy.16
  67.2 14.0 %all_gather.3.refs_4_ = bf16[1024,256]{1,0:T(8,128)(2,1)} all-gather(bf16[256,256]{1,0:T(8,128)(2,1)S(1)} %copy-done.3), channel_id=1, replica_groups=mesh['table'=4,'batch'=8] {'table'}, dimensions={0}, use_global_device_ids=true | all-gather | bytes 655360 | tf_op jit(solution)/shard_map/all_gather | solution.py:245
  81.2 15.9 %lookup.4 = (bf16[2048,256]{1,0:T(8,128)(2,1)}, bf16[2048,4096]{1,0:T(8,128)(2,1)}) custom-call(s32[2048,8]{1,0:T(8,128)} %bitcast.20, bf16[4096,256]{1,0:T(8,128)(2,1)} %multiply_convert_fusion.table_ref), custom_call_target="tpu_custom_call" | custom-call | flops 4294967296 | bytes 19922944 | tf_op jit(solution)/shard_map/lookup/pallas_call | solution.py:65
  97.1 0.0 collective-permute-done.2.refs_3_
  97.1 0.0 collective-permute-done.1.refs_2_
  97.1 0.0 copy-start.6
  97.1 0.0 collective-permute-done.refs_1_
  97.1 0.9 copy-done.5
  98.1 0.3 copy-done.6
  98.4 0.3 copy-done.7
  98.7 45.8 %samples.1 = (bf16[8,1024,256]{2,1,0:T(8,128)(2,1)}, bf16[8,256,256]{2,1,0:T(8,128)(2,1)}, bf16[8,256,256]{2,1,0:T(8,128)(2,1)}, bf16[8,256,256]{2,1,0:T(8,128)(...) custom-call(s32[1]{0:T(128)} %bitcast.me_ref, ...), custom_call_target="tpu_custom_call" | custom-call | flops 25769803776 | bytes 16777216 | tf_op jit(solution)/shard_map/samples/pallas_call | solution.py:160
  144.6 2.1 convert_element_type.18
  146.6 0.0 reduce-scatter.5.cloned.1.call-update
  146.6 0.0 all-reduce.4.cloned.1.call-start
  146.7 0.4 collective-permute-start.3
  147.1 2.3 collective-permute-start.4
  149.4 0.0 collective-permute-start.5
  149.4 24.0 %reduce-scatter.5.cloned.1.call-done = bf16[256,256]{1,0:T(8,128)(2,1)} async-done(((bf16[1024,256]{1,0:T(8,128)(2,1)}), bf16[256,256]{1,0:T(8,128)(2,1)}) %reduce-scatter.5.cloned.1.call-update) | async-done | bytes 131088 | tf_op jit(solution)/shard_map/reduce_scatter | solution.py:274
  173.5 0.0 all-reduce.4.cloned.1.call-update
  173.5 0.0 reduce-scatter.3.cloned.1.call-start
  173.5 0.0 collective-permute-done.3
  173.6 2.8 collective-permute-done.4
  176.4 21.6 %collective-permute-done.5 = bf16[8,256,256]{2,1,0:T(8,128)(2,1)S(1)} collective-permute-done((bf16[8,256,256]{2,1,0:T(8,128)(2,1)}, bf16[8,256,256]{2,1,0:T(8,128)(2,1)S(1)}, u32[]{:S(2)}, u32[]{:S(2)}) %collective-permute-start.5) | collective-permute-done | bytes 1048608 | tf_op jit(solution)/shard_map/ppermute | solution.py:247
  197.9 1.0 copy-done.2
  198.9 30.4 %scatter.1 = bf16[4096,256]{1,0:T(8,128)(2,1)} custom-call(bf16[2048,256]{1,0:T(8,128)(2,1)} %bitcast.15, bf16[2048,256]{1,0:T(8,128)(2,1)} %bitcast.16, bf16[2048,256]{1,0:T(8,128)(2,1)} %bitcast.17, bf16[2048,256]{1,0:T(8,128)(2,1)} %bitcast.18, bf16[2048,4096]{1,0:T(8,128)(2,1)} %get-tuple-element.34.refs_4_, ...), custom_call_target="tpu_custom_call" | custom-call | flops 17179869184 | bytes 71303168 | tf_op jit(solution)/shard_map/scatter/pallas_call | solution.py:210
  229.3 0.0 reduce-scatter.3.cloned.1.call-update
  229.3 0.0 all-reduce.6.cloned.1.call-start
  229.4 0.5 all-reduce.6.cloned.1.call-update
  229.9 41.0 %psum.36 = f32[256]{0:T(256)} all-reduce(f32[256]{0:T(256)S(1)} %bitcast.23), channel_id=1, replica_groups=mesh['table'=4,'batch'=8] {'table','batch'}, use_global_device_ids=true, to_apply=%region_3.0 | all-reduce | flops 256 | bytes 2048 | tf_op jit(solution)/shard_map/psum | solution.py:278
  270.9 1.6 convert_element_type.19
  272.6 45.0 %reduce-scatter.3.cloned.1.call-done = bf16[512,256]{1,0:T(8,128)(2,1)} async-done(((bf16[4096,256]{1,0:T(8,128)(2,1)}), bf16[512,256]{1,0:T(8,128)(2,1)}) %reduce-scatter.3.cloned.1.call-update) | async-done | bytes 262160 | tf_op jit(solution)/shard_map/reduce_scatter | solution.py:271
  317.5 1.8 convert_element_type.17
  319.3 136.2 %all-reduce.6.cloned.1.call-done = (f32[256,512]{1,0:T(8,128)}, f32[256,512]{1,0:T(8,128)}, f32[512,256]{1,0:T(8,128)}) async-done(((f32[256,512]{1,0:T(8,128)}, f32[256,512]{1,0:T(8,128)}, f32[512,256]{1,0:T(8,128)}), (f32[256,512]{1,0:T(8,128)}, f32[256,512]{1,0:T(8,128)}, f32[512,256]{1,0:T(8,128)})) %all-reduce.6.cloned.1.call-update) | async-done | bytes 1572880 | tf_op jit(solution)/shard_map/psum | solution.py:278
  455.5 1.9 copy.24
  457.4 1.9 copy.25
  459.3 1.9 copy.26
  (12 shorter events, 0.0 us)
Async XLA Ops:
  7.2 166.3 %reduce-scatter.5.cloned.1.call-start = ((), (), s32[]{:S(2)}) async-start(), calls=%async_computation.3 | async-start | bytes 655360 | tf_op jit(solution)/shard_map/reduce_scatter | solution.py:274
  28.3 68.8 %collective-permute-start.2 = (bf16[8,256,256]{2,1,0:T(8,128)(2,1)}, bf16[8,256,256]{2,1,0:T(8,128)(2,1)S(1)}, u32[]{:S(2)}, u32[]{:S(2)}) collective-permute-start(bf16[8,256,256]{2,1,0:T(8,128)(2,1)} %bitcast.24), channel_id=1, source_target_pairs={{0,24},{8,16},{16,8},{24,0},{1,25},{9,17},{17,9},{25,1},{2,26},{10... | collective-permute-start | bytes 3145736 | tf_op jit(solution)/shard_map/ppermute | solution.py:247
  47.9 49.1 %collective-permute-start.1 = (bf16[8,256,256]{2,1,0:T(8,128)(2,1)}, bf16[8,256,256]{2,1,0:T(8,128)(2,1)S(1)}, u32[]{:S(2)}, u32[]{:S(2)}) collective-permute-start(bf16[8,256,256]{2,1,0:T(8,128)(2,1)} %bitcast.25), channel_id=1, source_target_pairs={{0,16},{8,24},{16,0},{24,8},{1,17},{9,25},{17,1},{25,9},{2,18},{10... | collective-permute-start | bytes 3145736 | tf_op jit(solution)/shard_map/ppermute | solution.py:247
  49.8 17.4 %copy-start.3 = (bf16[256,256]{1,0:T(8,128)(2,1)S(1)}, bf16[256,256]{1,0:T(8,128)(2,1)}, u32[]{:S(2)}) copy-start(bf16[256,256]{1,0:T(8,128)(2,1)} %param.11) | copy-start | bytes 393220
  65.8 31.3 %collective-permute-start = (bf16[8,256,256]{2,1,0:T(8,128)(2,1)}, bf16[8,256,256]{2,1,0:T(8,128)(2,1)S(1)}, u32[]{:S(2)}, u32[]{:S(2)}) collective-permute-start(bf16[8,256,256]{2,1,0:T(8,128)(2,1)} %bitcast.26), channel_id=1, source_target_pairs={{0,8},{8,0},{16,24},{24,16},{1,9},{9,1},{17,25},{25,17},{2,10},{10... | collective-permute-start | bytes 3145736 | tf_op jit(solution)/shard_map/ppermute | solution.py:247
  97.1 1.0 copy-start.5
  97.1 1.3 copy-start.6
  97.1 1.6 copy-start.7
  146.6 124.3 %all-reduce.4.cloned.1.call-start = ((), (), s32[]{:S(2)}) async-start(), calls=%async_computation.4 | async-start | bytes 262144 | tf_op jit(solution)/shard_map/psum | solution.py:277
  146.7 26.8 %collective-permute-start.3 = (bf16[8,256,256]{2,1,0:T(8,128)(2,1)}, bf16[8,256,256]{2,1,0:T(8,128)(2,1)S(1)}, u32[]{:S(2)}, u32[]{:S(2)}) collective-permute-start(bf16[8,256,256]{2,1,0:T(8,128)(2,1)} %get-tuple-element.31), channel_id=1, source_target_pairs={{0,8},{8,0},{16,24},{24,16},{1,9},{9,1},{17,25},{25,17},{2,10},{10... | collective-permute-start | bytes 3145736 | tf_op jit(solution)/shard_map/ppermute | solution.py:247
  147.1 29.3 %collective-permute-start.4 = (bf16[8,256,256]{2,1,0:T(8,128)(2,1)}, bf16[8,256,256]{2,1,0:T(8,128)(2,1)S(1)}, u32[]{:S(2)}, u32[]{:S(2)}) collective-permute-start(bf16[8,256,256]{2,1,0:T(8,128)(2,1)} %get-tuple-element.32), channel_id=1, source_target_pairs={{0,16},{8,24},{16,0},{24,8},{1,17},{9,25},{17,1},{25,9},{2,18},{10... | collective-permute-start | bytes 3145736 | tf_op jit(solution)/shard_map/ppermute | solution.py:247
  149.4 48.5 %collective-permute-start.5 = (bf16[8,256,256]{2,1,0:T(8,128)(2,1)}, bf16[8,256,256]{2,1,0:T(8,128)(2,1)S(1)}, u32[]{:S(2)}, u32[]{:S(2)}) collective-permute-start(bf16[8,256,256]{2,1,0:T(8,128)(2,1)} %get-tuple-element.33), channel_id=1, source_target_pairs={{0,24},{8,16},{16,8},{24,0},{1,25},{9,17},{17,9},{25,1},{2,26},{10... | collective-permute-start | bytes 3145736 | tf_op jit(solution)/shard_map/ppermute | solution.py:247
  173.5 144.0 %reduce-scatter.3.cloned.1.call-start = ((), (), s32[]{:S(2)}) async-start(), calls=%async_computation.2 | async-start | bytes 2359296 | tf_op jit(solution)/shard_map/reduce_scatter | solution.py:271
  173.5 24.4 %copy-start = (bf16[8,256,256]{2,1,0:T(8,128)(2,1)}, bf16[8,256,256]{2,1,0:T(8,128)(2,1)S(1)}, u32[]{:S(2)}) copy-start(bf16[8,256,256]{2,1,0:T(8,128)(2,1)S(1)} %collective-permute-done.3) | copy-start | bytes 3145732
  176.4 21.6 %copy-start.1 = (bf16[8,256,256]{2,1,0:T(8,128)(2,1)}, bf16[8,256,256]{2,1,0:T(8,128)(2,1)S(1)}, u32[]{:S(2)}) copy-start(bf16[8,256,256]{2,1,0:T(8,128)(2,1)S(1)} %collective-permute-done.4) | copy-start | bytes 3145732
  197.9 1.0 copy-start.2
  198.9 31.0 %copy-start.4 = (f32[1,256]{1,0:T(1,128)S(1)}, f32[1,256]{1,0:T(1,128)}, u32[]{:S(2)}) copy-start(f32[1,256]{1,0:T(1,128)} %get-tuple-element.39) | copy-start | bytes 3076
  229.3 226.2 %all-reduce.6.cloned.1.call-start = ((), (), s32[]{:S(2)}) async-start(), calls=%async_computation.5 | async-start | bytes 3145728 | tf_op jit(solution)/shard_map/psum | solution.py:278
Sparse Core Ops, SparseCore 0:
  146.8 26.6 reduce-scatter.4
  177.2 69.6 all-reduce.3
  250.4 67.1 reduce-scatter.2
  323.6 131.9 all-reduce.5
